TPU v7x, 128 devices: a whole 4x4x4 slice. The times are simulated.
128 devices in a mesh: dp: 4 (over y_hi, core), fsdp: 32 (over z, y_lo, x).
Axes of the slice: x: 4, y: 4 (y_hi: 2, y_lo: 2; y = y_hi * 2 + y_lo), z: 4, core: 2. Of those that a mesh axis runs over, the one named last changes fastest.
Arguments:
- tokens: bfloat16 [2, 65536, 768], P(None, ('dp', 'fsdp')), may hold values from -6 to 6
- parts: int32 [2, 128, 8], P(None, ('dp', 'fsdp')), may hold values from 1 to 128, 512 in all within a row
- cotangent: bfloat16 [2, 65536, 768], P(None, ('dp', 'fsdp'))
- w_query: bfloat16 [768, 768], P(('dp', 'fsdp')), may hold values from -0.21875 to 0.21875
- w_key: bfloat16 [768, 768], P(('dp', 'fsdp')), may hold values from -0.21875 to 0.21875
- w_value: bfloat16 [768, 768], P(('dp', 'fsdp')), may hold values from -0.21875 to 0.21875
- w_out: bfloat16 [768, 768], P(('dp', 'fsdp')), may hold values from -0.625 to 0.625
- w_up: bfloat16 [768, 3072], P(('dp', 'fsdp')), may hold values from -0.21875 to 0.21875
- w_down: bfloat16 [3072, 768], P(('dp', 'fsdp')), may hold values from -0.109375 to 0.109375
- shared_a: bfloat16 [768, 1024], P(('dp', 'fsdp')), may hold values from -0.21875 to 0.21875
- shared_b: bfloat16 [1024, 768], P(('dp', 'fsdp')), may hold values from -0.1875 to 0.1875
- gain_one: float32 [768], replicated, may hold values from 0.1 to 1.9
- shift_one: float32 [768], replicated, may hold values from -1.5 to 1.5
- gain_two: float32 [768], replicated, may hold values from 0.1 to 1.9
- shift_two: float32 [768], replicated, may hold values from -1.5 to 1.5
- scale_dq: float32 [1024], replicated, may hold values from 0.3 to 1.5
- scale_bq: float32 [768], replicated, may hold values from -2.5 to 2.5
- scale_dv: float32 [1024], replicated, may hold values from 0.3 to 1.5
- scale_bv: float32 [768], replicated, may hold values from -2.5 to 2.5
Outputs:
- output: bfloat16 [2, 65536, 768], P(None, ('dp', 'fsdp'))
- grad_tokens: bfloat16 [2, 65536, 768], P(None, ('dp', 'fsdp'))
- grad_dq: float32 [1024], replicated
- grad_bq: float32 [768], replicated
- grad_dv: float32 [1024], replicated
- grad_bv: float32 [768], replicated
Inputs may be any that keep to these rules, and one draw needn't show every extreme that they name: `parts`: in every packed row the 4 pairs' two sentence lengths fill the row's 512 tokens exactly; entries 2p and 2p+1 are pair p's first and second sentence.
All inputs are finite; a program needn't handle non-finite values.
Results may differ from a plain program's by a relative error of at most 0.014.
Values may be sent and summed in bfloat16 or wider, within the bound.
A program may use at most 256 MiB of HBM per device.

v0:
```python
import jax
import jax.numpy as jnp
from jax import lax
from jax.experimental import pallas as pl
from jax.experimental.pallas import tpu as pltpu
from jax.sharding import PartitionSpec as P

MESH = pl.DeviceIdType.MESH
BF = jnp.bfloat16
F32 = jnp.float32


def place():
    dp = lax.axis_index("dp")
    fs = lax.axis_index("fsdp")
    return dict(x=fs % 4, y=(dp // 2) * 2 + (fs // 4) % 2, z=fs // 8, c=dp % 2)


def device(at):
    return ((at["y"] // 2) * 2 + at["c"], at["z"] * 8 + (at["y"] % 2) * 4 + at["x"])


def moved(at, axis, delta):
    size = 2 if axis == "c" else 4
    return {**at, axis: (at[axis] + delta + size) % size}


ORDERS = (("x", "y", "z"), ("y", "z", "x"), ("z", "x", "y"))
PEERS = 23


def near(at):
    for step in range(1, 8):
        x, yl = (at["x"] + step) % 4, (at["y"] + step // 4) % 2
        yield {**at, "x": x, "y": (at["y"] // 2) * 2 + yl}


def across(at):
    for step in range(1, 16):
        yh, c = (at["y"] // 2 + step // 8) % 2, (at["c"] + step // 4) % 2
        yield {**at, "y": yh * 2 + at["y"] % 2, "c": c, "z": (at["z"] + step) % 4}


def peers(at):
    return [*near(at), *across(at), {**at, "y": 3 - at["y"]}]


def enter_signal(at):
    for peer in peers(at):
        pl.semaphore_signal(pltpu.get_barrier_semaphore(), inc=1, device_id=device(peer), device_id_type=MESH)


def region(buf, kind, rot, done, at, low, high):
    every = slice(None)
    x, y, z, c = at["x"], at["y"], at["z"], at["c"]
    yh = every if "y" in done else y // 2
    yl = every if "y" in done else y % 2
    zs = every if "z" in done else z
    col = every if "x" in done else pl.ds(pl.multiple_of(x * 128, 128), 128)
    if kind == "panel":
        return buf.at[low:high, yl, yh, c, zs, rot, :, col]
    col = every if "x" in done else pl.ds(pl.multiple_of((x % 2) * 128, 128), 128)
    xh = every if "x" in done else x // 2
    if kind == "down":
        return buf.at[low:high, yh, c, zs, yl, xh, rot, :, col]
    return buf.at[rot, yh, c, zs, yl, xh, :, col]


class Moves:
    def __init__(self, at, bufs, send, recv):
        self.at, self.bufs, self.send, self.recv = at, bufs, send, recv
        self.slots = {}

    def slot(self, key):
        return self.slots.setdefault(key, len(self.slots))

    def copies(self, group, phase):
        kind, low, high = group
        buf = self.bufs[kind]
        for rot in range(3):
            order = ORDERS[rot]
            axis, done = order[phase], order[:phase]
            for delta in (1, 3, 2):
                k = self.slot((group, phase, rot, delta))
                yield (
                    region(buf, kind, rot, done, self.at, low, high),
                    moved(self.at, axis, delta),
                    region(buf, kind, rot, done, moved(self.at, axis, -delta), low, high),
                    k,
                )

    def sibling(self, group):
        kind, low, high = group
        buf = self.bufs[kind]
        k = self.slot((group, "c"))
        for here in (self.at,):
            other = moved(here, "c", 1)
            if kind == "panel":
                mine, theirs = buf.at[low:high, :, :, here["c"]], buf.at[low:high, :, :, other["c"]]
            elif kind == "up_b":
                mine, theirs = buf.at[:, :, here["c"]], buf.at[:, :, other["c"]]
            else:
                mine, theirs = buf.at[low:high, :, here["c"]], buf.at[low:high, :, other["c"]]
            yield mine, other, theirs, k

    def make(self, what):
        mine, target, theirs, k = what
        return pltpu.make_async_remote_copy(
            src_ref=mine,
            dst_ref=mine,
            send_sem=self.send.at[k],
            recv_sem=self.recv.at[k],
            device_id=device(target),
            device_id_type=MESH,
        )

    def arrival(self, what):
        mine, target, theirs, k = what
        return pltpu.make_async_remote_copy(
            src_ref=theirs,
            dst_ref=theirs,
            send_sem=self.send.at[k],
            recv_sem=self.recv.at[k],
            device_id=device(target),
            device_id_type=MESH,
        )

    def listed(self, group, phase):
        return self.sibling(group) if phase == 3 else self.copies(group, phase)

    def start(self, group, phase):
        for what in self.listed(group, phase):
            self.make(what).start()

    def wait(self, group, phase):
        for what in self.listed(group, phase):
            self.arrival(what).wait_recv()

    def sent(self, group, phase):
        for what in self.listed(group, phase):
            self.make(what).wait_send()


def stage_zero(at, shards, packed, landed, half_d, half_b, both_b, both_d, rows, bufs, send, recv):
    w_query, w_key, w_value, w_out, w_up, w_down, shared_a, shared_b = shards
    kvqo = (w_key, w_value, w_query, w_out)
    x, y, z, c = at["x"], at["y"], at["z"], at["c"]
    mine = (y % 2) * 4 + x

    def pick(ch, yl, dx):
        col = yl * 512 + dx * 128
        if ch == 0:
            return shared_a[:, col : col + 128]
        if ch < 4:
            start = (ch - 1) * 256 + col % 256
            return kvqo[col // 256][:, start : start + 128]
        start = (ch - 4) * 1024 + col
        return w_up[:, start : start + 128]

    for yl in range(2):
        for dx in range(4):
            for ch in range(7):
                packed[yl * 4 + dx, :, ch * 128 : ch * 128 + 128] = pick(ch, yl, dx)
    for odd in range(2):
        for r in range(3):
            tile = slice(r * 256 + odd * 128, r * 256 + odd * 128 + 128)
            both_b[odd, :, r * 128 : r * 128 + 128] = shared_b[:, tile]
            both_d[odd, :, r * 128 : r * 128 + 128] = w_down[:, tile]
    landed[pl.ds(mine, 1)] = packed[pl.ds(mine, 1)]
    pl.semaphore_wait(pltpu.get_barrier_semaphore(), PEERS)
    sends, arrivals = [], []
    for step in range(1, 8):
        dx, dy = step % 4, step // 4
        to = {**at, "x": (x + dx) % 4, "y": (y // 2) * 2 + (y + dy) % 2}
        fro = {**at, "x": (x - dx + 4) % 4, "y": (y // 2) * 2 + (y + dy) % 2}
        to_i, fro_i = (to["y"] % 2) * 4 + to["x"], (fro["y"] % 2) * 4 + fro["x"]
        sends.append(pltpu.make_async_remote_copy(
            src_ref=packed.at[to_i], dst_ref=landed.at[mine], send_sem=send.at[step], recv_sem=recv.at[step],
            device_id=device(to), device_id_type=MESH))
        arrivals.append(pltpu.make_async_remote_copy(
            src_ref=packed.at[to_i], dst_ref=landed.at[fro_i], send_sem=send.at[step], recv_sem=recv.at[step],
            device_id=device(to), device_id_type=MESH))
    other = {**at, "x": x + 1 - 2 * (x % 2)}
    for k, (src, dst) in enumerate(((both_d.at[1 - x % 2], half_d), (both_b.at[1 - x % 2], half_b))):
        sends.append(pltpu.make_async_remote_copy(
            src_ref=src, dst_ref=dst, send_sem=send.at[8 + k], recv_sem=recv.at[8 + k],
            device_id=device(other), device_id_type=MESH))
        arrivals.append(sends[-1])
    for copy in sends:
        copy.start()
    for copy in arrivals:
        copy.wait_recv()
    for i in range(8):
        rows[6 * i : 6 * i + 6, :] = landed[i].astype(F32)
    yh, yl = y // 2, y % 2
    block = rows[...].astype(BF).reshape(3, 16, 896)
    own = pl.ds(pl.multiple_of(x * 128, 128), 128)
    for ch in range(7):
        bufs["panel"][ch, yl, yh, c, z, :, :, own] = block[:, :, ch * 128 : ch * 128 + 128]
    lane = pl.ds(pl.multiple_of((x % 2) * 128, 128), 128)

    def joined(mine_too, got):
        a, b = mine_too.astype(F32), got[...].astype(F32)
        even = x % 2 == 0
        return jnp.concatenate([jnp.where(even, a, b), jnp.where(even, b, a)], axis=0).astype(BF)

    block = joined(both_d[x % 2], half_d).reshape(3, 16, 384)
    for k in range(3):
        bufs["down"][k, yh, c, z, yl, x // 2, :, :, lane] = block[:, :, k * 128 : k * 128 + 128]
    pair = joined(both_b[x % 2], half_b)
    for r in range(3):
        bufs["up_b"][r, yh, c, z, yl, x // 2, :, lane] = pair[:, r * 128 : r * 128 + 128]
    for copy in sends:
        copy.wait_send()


PANEL = (7, 2, 2, 2, 4, 3, 16, 512)
DOWN = (3, 2, 2, 4, 2, 2, 3, 16, 256)
UP_B = (3, 2, 2, 4, 2, 2, 16, 256)


LOG2E = 1.4426950408889634
SCALE_Q = 0.125 * LOG2E
NT = (((1,), (1,)), ((), ()))
TN = (((0,), (0,)), ((), ()))
NN = (((1,), (0,)), ((), ()))
FAR = -1e30
GRADS = ("hid", "slope")


def dot(left, right, dims=NN):
    return lax.dot_general(left, right, dims, preferred_element_type=F32)


def span(start, size):
    return pl.ds(pl.multiple_of(start, size), size)


def panel_of(s, ch, half, cols=slice(None)):
    part = s["panel"][ch, half, :, :, :, :, :, cols]
    return part.reshape(768, part.shape[-1])


def first_half(width=128):
    return lax.broadcasted_iota(jnp.int32, (1, width), 1) < 64


def rank_down(s):
    def half(hb, _):
        cols = span(hb * 512, 512)
        lat = dot(s["x"][...].reshape(1024, 768), panel_of(s, 0, hb))
        s["lat"][:, cols] = lat.astype(BF)
        for slot, name in ((8, "scale_dq"), (20, "scale_dv")):
            s["e"][pl.ds(slot + 2 * hb, 2)] = (lat * s[name][:, cols]).astype(BF).reshape(2, 512, 512)
        return 0

    lax.fori_loop(0, 2, half, 0)


def project(s, r):
    cols, base = slice(r * 256, r * 256 + 256), r * 768
    x = s["x"][...].reshape(1024, 768)
    s["qkv"][:, base : base + 256] = dot(x, panel_of(s, 1 + r, 0, slice(0, 256))).astype(BF)
    for slot, half, off, scale, kept, at, factor in (
        (20, 0, 256, "scale_bv", "vt", 256, None),
        (8, 1, 0, "scale_bq", "qt", 512, SCALE_Q),
    ):
        low, high = (s["e"][slot + 2 * hb : slot + 2 * hb + 2].reshape(1024, 512) for hb in range(2))
        up = s["up_b"][r].reshape(1024, 256)
        t = dot(low, up[:512]) + dot(high, up[512:])
        s[kept][:, cols] = t.astype(BF)
        full = dot(x, panel_of(s, 1 + r, half, slice(off, off + 256))) + s[scale][:, cols] * t
        s["qkv"][:, base + at : base + at + 256] = (full * factor if factor else full).astype(BF)


def masks(s):
    def micro(m, _):
        pos = lax.broadcasted_iota(jnp.int32, (512, 128), 0)
        lane = lax.broadcasted_iota(jnp.int32, (512, 128), 1) % 64
        end = jnp.int32(0)
        pair = jnp.zeros((512, 128), jnp.int32)
        for p in range(4):
            end = end + s["parts"][m, 0, 2 * p] + s["parts"][m, 0, 2 * p + 1]
            pair = pair + (pos >= end).astype(jnp.int32)
        own = lane == pair
        s["mq"][m] = jnp.where(own, 1.0, 0.0).astype(BF)
        s["mk"][m] = jnp.where(own | (lane >= 8), 0.0, FAR).astype(BF)
        return 0

    lax.fori_loop(0, 2, micro, 0)


def places(r, i):
    m, half = i // 2, i % 2
    base = r * 768 + half * 128
    kvq = [span(base + j * 256, 128) for j in range(3)]
    return m, 2 * r + half, span(m * 512, 512), kvq, span(r * 256 + half * 128, 128)


def scores(s, buf, r, i, h):
    m, _, rows, (kc, _, qc), _ = places(r, i)
    mine = first_half() if h == 0 else ~first_half()
    k = jnp.where(mine, s["qkv"][rows, kc], s["mk"][m])
    q = jnp.where(mine, s["qkv"][rows, qc], s["mq"][m])
    buf[:, :512] = dot(q, k, NT)


def mix(s, buf, r, i, h):
    m, p, rows, (_, vc, _), _ = places(r, i)
    mine = first_half() if h == 0 else ~first_half()
    v = s["qkv"][rows, vc]
    sc = buf[:, :512]
    e = jnp.exp2(sc - jnp.max(sc, axis=1, keepdims=True)).astype(BF)
    s["e"][m * 12 + 2 * p + h] = e
    return dot(e, jnp.where(mine, v, jnp.ones_like(v)))


def attend(s, r):
    s_a, s_b = s["f_a"], s["g_one"].at[0:512, :]
    scores(s, s_a, r, 0, 0)

    def pair(i, _):
        _, _, rows, _, cols = places(r, i)
        scores(s, s_b, r, i, 1)
        o0 = mix(s, s_a, r, i, 0)
        scores(s, s_a, r, jnp.minimum(i + 1, 3), 0)
        o1 = mix(s, s_b, r, i, 1)
        total = pltpu.roll(jnp.where(first_half(), o1, o0), 64, 1)
        inverse = 1.0 / total
        s["inv"][rows, cols] = inverse.astype(BF)
        s["att"][rows, cols] = (jnp.where(first_half(), o0, o1) * inverse).astype(BF)
        return 0

    lax.fori_loop(0, 4, pair, 0, unroll=4)


def mean(v):
    return jnp.mean(v, axis=1, keepdims=True)


def norm(v):
    centred = v - mean(v)
    r = lax.rsqrt(mean(centred * centred) + 1e-05)
    return centred * r, r


def norm_back(hat, r, g):
    return r * (g - mean(g) - hat * mean(g * hat))


def by_rows(fn, size=128):
    for start in range(0, 512, size):
        fn(slice(start, start + size))


def middle(s, m, hooks=None):
    rows = span(m * 512, 512)
    hat, hid, slope = s["f_a"], s["hid"], s["slope"]
    other, low, inv = s["g_one"].at[rows, :], s["ga"].at[rows, :], s["inv"].at[rows, :]
    x, cot = s["x"].at[m], s["cot"].at[m]
    att = s["att"][rows, :]
    for r in range(3):
        hat[:, r * 256 : r * 256 + 256] = dot(att, panel_of(s, 1 + r, 1, slice(256, 512)))

    def norm_one(r):
        n, r1 = norm(x[r, :].astype(F32) + hat[r, :])
        hat[r, :] = n
        low[r, :] = (n * s["gain_one"][...] + s["shift_one"][...]).astype(BF)
        s["r1"][r, :] = r1

    by_rows(norm_one)

    if hooks:
        hooks[0]()
    for t in range(6):
        if hooks and t in hooks[2]:
            hooks[2][t]()
        u = dot(low[...], panel_of(s, 4 + t // 2, t % 2))
        cdf = 0.5 + 0.5 * lax.erf(u * 0.7071067811865476)
        cols = span(t * 512, 512)
        hid[:, cols] = (u * cdf).astype(BF)
        slope[:, cols] = (cdf + (u * 0.3989422804014327) * jnp.exp2(u * (u * (-0.5 * LOG2E)))).astype(BF)
    if hooks:
        hooks[1]()
    for k in range(3):
        other[:, k * 256 : k * 256 + 256] = dot(hid[...], s["down"][k].reshape(3072, 256))

    def norm_two(r):
        n2, r2 = norm(hat[r, :] * s["gain_one"][...] + s["shift_one"][...] + other[r, :])
        x[r, :] = (n2 * s["gain_two"][...] + s["shift_two"][...]).astype(BF)
        g = norm_back(n2, r2, cot[r, :].astype(F32) * s["gain_two"][...])
        other[r, :] = g
        low[r, :] = g.astype(BF)

    by_rows(norm_two)

    def back(t, _):
        cols = span(t * 768, 768)
        g = sum(dot(low[:, k * 256 : k * 256 + 256], s["down"][k, t // 2, t % 2].reshape(768, 256), NT) for k in range(3))
        hid[:, cols] = (g * slope[:, cols].astype(F32)).astype(BF)
        return 0

    lax.fori_loop(0, 4, back, 0, unroll=4)

    other[...] += sum(dot(hid[:, t * 512 : t * 512 + 512], panel_of(s, 4 + t // 2, t % 2), NT) for t in range(6))

    def norm_one_back(r):
        g = norm_back(hat[r, :], s["r1"][r, :], other[r, :] * s["gain_one"][...])
        other[r, :] = g
        low[r, :] = g.astype(BF)

    by_rows(norm_one_back)
    hat[...] = sum(dot(low[:, r * 256 : r * 256 + 256], panel_of(s, 1 + r, 1, slice(256, 512)), NT) for r in range(3))

    def scale_att(r):
        low[r, :] = (hat[r, :] * inv[r, :].astype(F32)).astype(BF)

    by_rows(scale_att)


def attend_back(s):
    def third(r, _):
        for i in range(4):
            m, p, rows, (kc, vc, qc), cols = places(r, i)
            k, v, q = s["qkv"][rows, kc], s["qkv"][rows, vc], s["qkv"][rows, qc]
            ga = s["ga"][rows, cols]
            prod = ga.astype(F32) * s["att"][rows, cols].astype(F32)
            gq = gk = gv = None
            lanes = lax.broadcasted_iota(jnp.int32, (1, 128), 1)
            for h in range(2):
                mine = first_half() if h == 0 else ~first_half()
                delta = -jnp.sum(jnp.where(mine, prod, 0.0), axis=1, keepdims=True)
                high = delta.astype(BF)
                rest = (delta - high.astype(F32)).astype(BF)
                zero = jnp.zeros_like(ga)
                gah = jnp.where(mine, ga, zero)
                aug = jnp.where(mine, ga, jnp.where(lanes % 64 == 0, high, jnp.where(lanes % 64 == 1, rest, zero)))
                gp = dot(aug, jnp.where(mine, v, jnp.ones_like(v)), NT)
                e = s["e"][m * 12 + 2 * p + h]
                gs = (e.astype(F32) * gp).astype(BF)
                gvh = dot(e, gah, TN)
                gqh = dot(gs, jnp.where(mine, k, zero))
                gkh = dot(gs, jnp.where(mine, q, zero), TN)
                gq, gk, gv = (gqh, gkh, gvh) if h == 0 else (gq + gqh, gk + gkh, gv + gvh)
            to = s[GRADS[m]]
            to[:, qc] = (gq * 0.125).astype(BF)
            to[:, kc] = (gk * (1.0 / LOG2E)).astype(BF)
            to[:, vc] = gv.astype(BF)
        return 0

    lax.fori_loop(0, 3, third, 0)


def vera_back(s):
    for base, kept, scale, row, keep in ((512, "qt", "scale_bq", 1, "att"), (256, "vt", "scale_bv", 3, "ga")):
        for r in range(3):
            cols = slice(r * 256, r * 256 + 256)

            total = jnp.zeros((1, 256), F32)
            for m in range(2):
                rows = slice(m * 512, m * 512 + 512)
                g = s[GRADS[m]][:, r * 768 + base : r * 768 + base + 256].astype(F32)
                s[keep][rows, cols] = (g * s[scale][:, cols]).astype(BF)
                total = total + jnp.sum(g * s[kept][rows, cols].astype(F32), axis=0, keepdims=True)
            s["red"][row : row + 1, cols] = total

    def half(hb, _):
        cols = span(hb * 512, 512)
        for m in range(2):
            rows = slice(m * 512, m * 512 + 512)
            gqu, gvu = (
                sum(dot(s[name][rows, r * 256 : r * 256 + 256], s["up_b"][r, hb].reshape(512, 256), NT) for r in range(3))
                for name in ("att", "ga")
            )
            lat = s["lat"][rows, cols].astype(F32)
            for row, val in ((0, gqu), (2, gvu)):
                part = jnp.sum(val * lat, axis=0, keepdims=True)
                if m:
                    part = part + s["red"][row : row + 1, cols]
                s["red"][row : row + 1, cols] = part
            s["e"][2 * hb + m] = (gqu * s["scale_dq"][:, cols] + gvu * s["scale_dv"][:, cols]).astype(BF)
        return 0

    lax.fori_loop(0, 2, half, 0)


def token_grads(s, m):
    rows = slice(m * 512, m * 512 + 512)
    terms = []
    for r in range(3):
        for j, (half, off) in enumerate(((0, 0), (0, 256), (1, 0))):
            lo = r * 768 + j * 256
            terms.append(dot(s[GRADS[m]][:, lo : lo + 256], panel_of(s, 1 + r, half, slice(off, off + 256)), NT))
    for hb in range(2):
        terms.append(dot(s["e"][2 * hb + m], panel_of(s, 0, hb), NT))
    s["cot"][m] = (s["g_one"][rows, :] + sum(terms)).astype(BF)


LAYER_SCRATCH = dict(
    panel=(PANEL, BF),
    down=(DOWN, BF),
    up_b=(UP_B, BF),
    x=((2, 512, 768), BF),
    cot=((2, 512, 768), BF),
    lat=((1024, 1024), BF),
    qt=((1024, 768), BF),
    vt=((1024, 768), BF),
    qkv=((1024, 2304), BF),
    e=((24, 512, 512), BF),
    att=((1024, 768), BF),
    inv=((1024, 768), BF),
    ga=((1024, 768), BF),
    g_one=((1024, 768), F32),
    f_a=((512, 768), F32),
    hid=((512, 3072), BF),
    slope=((512, 3072), BF),
    mq=((2, 512, 128), BF),
    mk=((2, 512, 128), BF),
    r1=((512, 1), F32),
    red=((4, 1024), F32),
)


VECTORS = ("gain_one", "shift_one", "gain_two", "shift_two", "scale_dq", "scale_bq", "scale_dv", "scale_bv")
SHARDS = ("w_query", "w_key", "w_value", "w_out", "w_up", "w_down", "shared_a", "shared_b")
SHARD_SHAPES = ((6, 768),) * 4 + ((6, 3072), (24, 768), (6, 1024), (8, 768))
GROUP_A, GROUP_1, GROUP_2, GROUP_3, UP_0, UP_1, UP_2 = (("panel", i, i + 1) for i in range(7))
DOWN_0, DOWN_1, DOWN_2 = (("down", i, i + 1) for i in range(3))
GROUP_B, FRONT, GROUP_UP, GROUP_DOWN = ("up_b", 0, 3), ("panel", 0, 4), ("panel", 4, 7), ("down", 0, 3)
LATE = (GROUP_UP, GROUP_DOWN)


def near_place(at):
    return (at["y"] % 2) * 4 + at["x"]


def across_place(at):
    return 8 + ((at["y"] // 2) * 2 + at["c"]) * 4 + at["z"]


def reduce_start(at, group, place_of, s, send, recv):
    here = place_of(at)
    s["sums"][pl.ds(here, 1)] = s["red"][...][None]
    sends, arrivals = [], []
    for i, other in enumerate(group(at)):
        k = i if place_of is near_place else 7 + i
        for found, slot in ((sends, here), (arrivals, place_of(other))):
            found.append(pltpu.make_async_remote_copy(
                src_ref=s["sums"].at[here], dst_ref=s["sums"].at[slot],
                send_sem=send.at[k], recv_sem=recv.at[place_of(other)] if found is arrivals else recv.at[here],
                device_id=device(other), device_id_type=MESH))
    for copy in sends:
        copy.start()
    return sends, arrivals


def reduce_end(state, first, size, s):
    sends, arrivals = state
    for copy in arrivals:
        copy.wait_recv()
    for copy in sends:
        copy.wait_send()
    values = [s["sums"][first + i] for i in range(size)]
    while len(values) > 1:
        values = [values[i] + values[i + 1] for i in range(0, len(values), 2)]
    s["red"][...] = values[0]


EXTRA = dict(
    packed=((8, 6, 896), BF),
    landed=((8, 6, 896), BF),
    half_d=((24, 384), BF),
    half_b=((8, 384), BF),
    both_b=((2, 8, 384), BF),
    both_d=((2, 24, 384), BF),
    rows=((48, 896), F32),
    sums=((24, 4, 1024), F32),
)


def whole(*refs):
    names = ("tokens", "parts_in", "cotangent") + tuple("in_" + n for n in SHARDS) + tuple("in_" + n for n in VECTORS)
    names += ("out", "grad_tokens", "grad_dq", "grad_bq", "grad_dv", "grad_bv")
    scratch = tuple(LAYER_SCRATCH) + tuple(EXTRA) + SHARDS + VECTORS
    names += scratch + ("parts", "loads", "send_0", "recv_0", "send", "recv", "send_r", "recv_r")
    s = dict(zip(names, refs, strict=True))
    at = place()
    enter_signal(at)
    loads = []
    pairs = [(s["in_" + n], s[n]) for n in SHARDS] + [(s["in_" + n], s[n].at[0]) for n in VECTORS]
    pairs += [(s["parts_in"], s["parts"]), (s["tokens"], s["x"]), (s["cotangent"], s["cot"])]
    for i, (src, dst) in enumerate(pairs):
        loads.append(pltpu.make_async_copy(src, dst, s["loads"].at[i]))
        loads[-1].start()
    for copy in loads[:8]:
        copy.wait()
    bufs = {k: s[k] for k in ("panel", "down", "up_b")}
    stage_zero(at, [s[n] for n in SHARDS], s["packed"], s["landed"], s["half_d"], s["half_b"], s["both_b"], s["both_d"], s["rows"], bufs, s["send_0"], s["recv_0"])
    moves = Moves(at, bufs, s["send"], s["recv"])
    begun = []

    def start(group, phase):
        moves.start(group, phase)
        begun.append((group, phase))

    def pass_on(group):
        moves.wait(group, 2)
        start(group, 3)

    def before_up():
        for group in (UP_0, UP_1, UP_2):
            moves.wait(group, 3)

    def before_down():
        for group in (DOWN_0, DOWN_1, DOWN_2):
            moves.wait(group, 3)

    hooks = (before_up, before_down, {i + 3: lambda g=g: pass_on(g) for i, g in enumerate((DOWN_0, DOWN_1, DOWN_2))})

    start(FRONT, 0)
    start(GROUP_B, 0)
    for group in LATE:
        start(group, 0)
    moves.wait(FRONT, 0)
    start(FRONT, 1)
    moves.wait(GROUP_B, 0)
    start(GROUP_B, 1)
    for group in LATE:
        moves.wait(group, 0)
        start(group, 1)
    moves.wait(FRONT, 1)
    start(GROUP_A, 2)
    start(GROUP_1, 2)
    moves.wait(GROUP_B, 1)
    start(GROUP_B, 2)
    start(GROUP_2, 2)
    for copy in loads[8:]:
        copy.wait()
    masks(s)
    pass_on(GROUP_A)
    start(GROUP_3, 2)
    moves.wait(GROUP_UP, 1)
    start(UP_0, 2)
    moves.wait(GROUP_A, 3)
    rank_down(s)
    pass_on(GROUP_1)
    pass_on(GROUP_B)
    start(UP_1, 2)
    start(UP_2, 2)
    moves.wait(GROUP_1, 3)
    moves.wait(GROUP_B, 3)
    project(s, 0)
    pass_on(GROUP_2)
    moves.wait(GROUP_DOWN, 1)
    start(DOWN_0, 2)
    attend(s, 0)
    pass_on(GROUP_3)
    start(DOWN_1, 2)
    moves.wait(GROUP_2, 3)
    project(s, 1)
    start(DOWN_2, 2)
    attend(s, 1)
    pass_on(UP_0)
    moves.wait(GROUP_3, 3)
    project(s, 2)
    pass_on(UP_1)
    attend(s, 2)
    pass_on(UP_2)
    middle(s, 0, hooks)
    middle(s, 1)
    result = pltpu.make_async_copy(s["x"], s["out"], s["loads"].at[0])
    result.start()
    for group, phase in begun:
        moves.sent(group, phase)
    attend_back(s)
    vera_back(s)
    for row in (1, 3):
        s["red"][row : row + 1, 768:1024] = jnp.zeros((1, 256), F32)
    state = reduce_start(at, near, near_place, s, s["send_r"], s["recv_r"])
    token_grads(s, 0)
    reduce_end(state, 0, 8, s)
    state = reduce_start(at, across, across_place, s, s["send_r"], s["recv_r"])
    token_grads(s, 1)
    ends = [result]
    ends.append(pltpu.make_async_copy(s["cot"], s["grad_tokens"], s["loads"].at[1]))
    ends[-1].start()
    reduce_end(state, 8, 16, s)
    for i, name in enumerate(("grad_dq", "grad_bq", "grad_dv", "grad_bv")):
        ends.append(pltpu.make_async_copy(s["red"].at[i, 0 : s[name].shape[0]], s[name], s["loads"].at[2 + i]))
        ends[-1].start()
    assert len(moves.slots) == 182
    assert len(moves.slots) == 182
    for copy in ends:
        copy.wait()


def hand_over(*refs):
    sources, results, held, sems = refs[:6], refs[6:12], refs[12:18], refs[18:]
    pieces = []
    for i, (src, dst, mid) in enumerate(zip(sources, results, held, strict=True)):
        if i < 2:
            pieces += [[a.at[m, r : r + 256] for a in (src, mid, dst)] for m in range(2) for r in (0, 256)]
        else:
            pieces.append([src, mid, dst])
    ins = [pltpu.make_async_copy(a, b, sems[0].at[k]) for k, (a, b, _) in enumerate(pieces)]
    outs = [pltpu.make_async_copy(b, c, sems[1].at[k]) for k, (_, b, c) in enumerate(pieces)]
    for copy in ins:
        copy.start()
    for before, after in zip(ins, outs, strict=True):
        before.wait()
        after.start()
    for copy in outs:
        copy.wait()


def shards(tokens, parts, cotangent, *rest):
    anywhere = pl.BlockSpec(memory_space=pl.ANY)
    scratch = [pltpu.VMEM(shape, kind) for shape, kind in (*LAYER_SCRATCH.values(), *EXTRA.values())]
    scratch += [pltpu.VMEM(shape, BF) for shape in SHARD_SHAPES]
    scratch += [pltpu.VMEM((1, v.shape[0]), F32) for v in rest[8:]]
    scratch += [pltpu.SMEM((2, 1, 8), jnp.int32)]
    scratch += [pltpu.SemaphoreType.DMA((n,)) for n in (19, 10, 10, 182, 182, 22, 24)]
    shapes = [jax.ShapeDtypeStruct((2, 512, 768), BF)] * 2
    shapes += [jax.ShapeDtypeStruct((n,), F32) for n in (1024, 768, 1024, 768)]
    found = pl.pallas_call(
        whole,
        out_shape=shapes,
        in_specs=[anywhere] * 19,
        out_specs=[anywhere] * 6,
        scratch_shapes=scratch,
        compiler_params=pltpu.CompilerParams(collective_id=0, has_side_effects=True, vmem_limit_bytes=66900000),
    )(tokens, parts, cotangent, *rest)
    held = [pltpu.VMEM(shape.shape, shape.dtype) for shape in shapes]
    return tuple(pl.pallas_call(
        hand_over,
        out_shape=shapes,
        in_specs=[anywhere] * 6,
        out_specs=[anywhere] * 6,
        scratch_shapes=held + [pltpu.SemaphoreType.DMA((12,))] * 2,
        compiler_params=pltpu.CompilerParams(vmem_limit_bytes=8 << 20),
    )(*found))


def solution(mesh):
    rows, split, same = P(None, ("dp", "fsdp"), None), P(("dp", "fsdp"), None), P()
    return jax.shard_map(
        shards,
        mesh=mesh,
        in_specs=(rows,) * 3 + (split,) * 8 + (same,) * 8,
        out_specs=(rows, rows, same, same, same, same),
        check_vma=False,
    )
```

profile of v0, /device:TPU:1, one launch (start us, length us, event | category | flops | bytes accessed | tf_op | source)
XLA Modules:
  0.0 139.6 jit_solution(17183651507686140878)
XLA Ops:
  0.6 129.8 %shard_map.226 = (bf16[2,512,768]{2,1,0:T(8,128)(2,1)}, bf16[2,512,768]{2,1,0:T(8,128)(2,1)}, f32[1024]{0:T(1024)}, f32[768]{0:T(1024)}, f32[1024]{0:T(1024)}, /*index=5*/f32[768]{0:T(1024)}) custom-call(bf16[2,512,768]{2,1,0:T(8,128)(2,1)} %refs_0_.1, s32[2,1,8]{2,1,0:T(1,128)} %refs_1_.1, bf16[2,512,768]{2,1,0:T(8,128)(2,1)} %refs_2_.1, ...), custom_call_target="tpu_custom_call" | custom-call | tf_op jit(solution)/shard_map/pallas_call | solution.py:725
  130.5 0.0 copy-start
  130.5 1.4 %copy-done = bf16[2,512,768]{2,1,0:T(8,128)(2,1)S(1)} copy-done((bf16[2,512,768]{2,1,0:T(8,128)(2,1)S(1)}, bf16[2,512,768]{2,1,0:T(8,128)(2,1)}, u32[]{:S(2)}) %copy-start) | copy-done | bytes 1572888
  131.9 0.0 copy-start.1
  131.9 1.4 %copy-done.1 = bf16[2,512,768]{2,1,0:T(8,128)(2,1)S(1)} copy-done((bf16[2,512,768]{2,1,0:T(8,128)(2,1)S(1)}, bf16[2,512,768]{2,1,0:T(8,128)(2,1)}, u32[]{:S(2)}) %copy-start.1) | copy-done | bytes 1572888
  133.3 0.0 copy-start.2
  133.3 0.7 copy-done.2
  134.0 0.0 copy-start.3
  134.0 0.7 copy-done.3
  134.6 0.0 copy-start.4
  134.7 0.7 copy-done.4
  135.3 0.0 copy-start.5
  135.3 0.7 copy-done.5
  136.0 3.4 %shard_map.227 = (bf16[2,512,768]{2,1,0:T(8,128)(2,1)}, bf16[2,512,768]{2,1,0:T(8,128)(2,1)}, f32[1024]{0:T(1024)}, f32[768]{0:T(1024)}, f32[1024]{0:T(1024)}, /*index=5*/f32[768]{0:T(1024)}) custom-call(bf16[2,512,768]{2,1,0:T(8,128)(2,1)S(1)} %copy-done, bf16[2,512,768]{2,1,0:T(8,128)(2,1)S(1)} %copy-done.1, f32[1024]{0:T(1024)S(1)} %copy-done.2, ...), custom_call_target="tpu_custom_call" | custom-call | tf_op jit(solution)/shard_map/pallas_call | solution.py:734
Async XLA Ops:
  130.5 1.4 %copy-start = (bf16[2,512,768]{2,1,0:T(8,128)(2,1)S(1)}, bf16[2,512,768]{2,1,0:T(8,128)(2,1)}, u32[]{:S(2)}) copy-start(bf16[2,512,768]{2,1,0:T(8,128)(2,1)} %get-tuple-element.12.refs_0_) | copy-start | bytes 4718596
  131.9 1.4 %copy-start.1 = (bf16[2,512,768]{2,1,0:T(8,128)(2,1)S(1)}, bf16[2,512,768]{2,1,0:T(8,128)(2,1)}, u32[]{:S(2)}) copy-start(bf16[2,512,768]{2,1,0:T(8,128)(2,1)} %get-tuple-element.13.refs_1_) | copy-start | bytes 4718596
  133.3 0.7 copy-start.2
  134.0 0.7 copy-start.3
  134.6 0.7 copy-start.4
  135.3 0.7 copy-start.5
where the time goes:
time: 142 us; the launch traced here: 140 us
  Pallas kernels  133 us (94%)
  local copies, waits for them, and re-layouts  5.49 us (4%)
    pallas_call x1, Pallas kernels, shards(): pl.pallas_call(whole, out_shape=shapes, in_specs=[anywhere] * 19, out_spe...  130 us
    unnamed x12, local copies, waits for them, and re-layouts  5.49 us
    pallas_call x1, Pallas kernels, shards(): pl.pallas_call(hand_over, out_shape=shapes, in_specs=[anywhere] * 6, out_...  3.37 us

commit v1 on v0

--- a/solution.py
+++ b/solution.py
@@ -80,7 +80,7 @@
         for rot in range(3):
             order = ORDERS[rot]
             axis, done = order[phase], order[:phase]
-            for delta in (1, 3, 2):
+            for delta in (2, 1, 3):
                 k = self.slot((group, phase, rot, delta))
                 yield (
                     region(buf, kind, rot, done, self.at, low, high),
@@ -678,11 +678,13 @@
         s["red"][row : row + 1, 768:1024] = jnp.zeros((1, 256), F32)
     state = reduce_start(at, near, near_place, s, s["send_r"], s["recv_r"])
     token_grads(s, 0)
+    ends = [result]
+    ends.append(pltpu.make_async_copy(s["cot"].at[0], s["grad_tokens"].at[0], s["loads"].at[1]))
+    ends[-1].start()
     reduce_end(state, 0, 8, s)
     state = reduce_start(at, across, across_place, s, s["send_r"], s["recv_r"])
     token_grads(s, 1)
-    ends = [result]
-    ends.append(pltpu.make_async_copy(s["cot"], s["grad_tokens"], s["loads"].at[1]))
+    ends.append(pltpu.make_async_copy(s["cot"].at[1], s["grad_tokens"].at[1], s["loads"].at[6]))
     ends[-1].start()
     reduce_end(state, 8, 16, s)
     for i, name in enumerate(("grad_dq", "grad_bq", "grad_dv", "grad_bv")):
@@ -737,7 +739,7 @@
         in_specs=[anywhere] * 6,
         out_specs=[anywhere] * 6,
         scratch_shapes=held + [pltpu.SemaphoreType.DMA((12,))] * 2,
-        compiler_params=pltpu.CompilerParams(vmem_limit_bytes=8 << 20),
+        compiler_params=pltpu.CompilerParams(vmem_limit_bytes=66900000),
     )(*found))
 
 

time: 142 us -> 136 us (0.958)
  local copies, waits for them, and re-layouts: 5.49 us -> 0 us
    unnamed x12 -> x0, local copies, waits for them, and re-layouts: 5.49 us -> none
where the time goes in v1:
time: 136 us; the launch traced here: 133 us
  Pallas kernels  132 us (97%)
    pallas_call x1, Pallas kernels, shards(): pl.pallas_call(whole, out_shape=shapes, in_specs=[anywhere] * 19, out_spe...  130 us
    pallas_call x1, Pallas kernels, shards(): pl.pallas_call(hand_over, out_shape=shapes, in_specs=[anywhere] * 6, out_...  2.87 us

profile of v1, /device:TPU:1, one launch (start us, length us, event | category | flops | bytes accessed | tf_op | source)
XLA Modules:
  0.0 133.3 jit_solution(11326015696884931622)
XLA Ops:
  0.6 129.6 %shard_map.226 = (bf16[2,512,768]{2,1,0:T(8,128)(2,1)}, bf16[2,512,768]{2,1,0:T(8,128)(2,1)}, f32[1024]{0:T(1024)}, f32[768]{0:T(1024)}, f32[1024]{0:T(1024)}, /*index=5*/f32[768]{0:T(1024)}) custom-call(bf16[2,512,768]{2,1,0:T(8,128)(2,1)} %refs_0_.1, s32[2,1,8]{2,1,0:T(1,128)} %refs_1_.1, bf16[2,512,768]{2,1,0:T(8,128)(2,1)} %refs_2_.1, ...), custom_call_target="tpu_custom_call" | custom-call | tf_op jit(solution)/shard_map/pallas_call | solution.py:727
  130.2 2.9 %shard_map.227 = (bf16[2,512,768]{2,1,0:T(8,128)(2,1)}, bf16[2,512,768]{2,1,0:T(8,128)(2,1)}, f32[1024]{0:T(1024)}, f32[768]{0:T(1024)}, f32[1024]{0:T(1024)}, /*index=5*/f32[768]{0:T(1024)}) custom-call(bf16[2,512,768]{2,1,0:T(8,128)(2,1)} %get-tuple-element.12.refs_0_, bf16[2,512,768]{2,1,0:T(8,128)(2,1)} %get-tuple-element.13.refs_1_, ...), custom_call_target="tpu_custom_call" | custom-call | tf_op jit(solution)/shard_map/pallas_call | solution.py:736

commit v2 on v1

--- a/solution.py
+++ b/solution.py
@@ -257,10 +257,14 @@
     lax.fori_loop(0, 2, half, 0)
 
 
+def project_keys(s, r):
+    x = s["x"][...].reshape(1024, 768)
+    s["qkv"][:, r * 768 : r * 768 + 256] = dot(x, panel_of(s, 1 + r, 0, slice(0, 256))).astype(BF)
+
+
 def project(s, r):
     cols, base = slice(r * 256, r * 256 + 256), r * 768
     x = s["x"][...].reshape(1024, 768)
-    s["qkv"][:, base : base + 256] = dot(x, panel_of(s, 1 + r, 0, slice(0, 256))).astype(BF)
     for slot, half, off, scale, kept, at, factor in (
         (20, 0, 256, "scale_bv", "vt", 256, None),
         (8, 1, 0, "scale_bq", "qt", 512, SCALE_Q),
@@ -619,21 +623,21 @@
 
     start(FRONT, 0)
     start(GROUP_B, 0)
-    for group in LATE:
-        start(group, 0)
     moves.wait(FRONT, 0)
     start(FRONT, 1)
     moves.wait(GROUP_B, 0)
     start(GROUP_B, 1)
     for group in LATE:
-        moves.wait(group, 0)
-        start(group, 1)
+        start(group, 0)
     moves.wait(FRONT, 1)
     start(GROUP_A, 2)
     start(GROUP_1, 2)
     moves.wait(GROUP_B, 1)
     start(GROUP_B, 2)
     start(GROUP_2, 2)
+    for group in LATE:
+        moves.wait(group, 0)
+        start(group, 1)
     for copy in loads[8:]:
         copy.wait()
     masks(s)
@@ -648,6 +652,7 @@
     start(UP_1, 2)
     start(UP_2, 2)
     moves.wait(GROUP_1, 3)
+    project_keys(s, 0)
     moves.wait(GROUP_B, 3)
     project(s, 0)
     pass_on(GROUP_2)
@@ -657,11 +662,13 @@
     pass_on(GROUP_3)
     start(DOWN_1, 2)
     moves.wait(GROUP_2, 3)
+    project_keys(s, 1)
     project(s, 1)
     start(DOWN_2, 2)
     attend(s, 1)
     pass_on(UP_0)
     moves.wait(GROUP_3, 3)
+    project_keys(s, 2)
     project(s, 2)
     pass_on(UP_1)
     attend(s, 2)

time: 136 us -> 142 us (1.044)
  Pallas kernels: 132 us -> 139 us
    pallas_call x1, Pallas kernels: 130 us -> 136 us  [shards(): pl.pallas_call(whole, out_shape=shapes, in_specs=[anywhere] * 19, out_spe...]
where the time goes in v2:
time: 142 us; the launch traced here: 140 us
  Pallas kernels  139 us (98%)
    pallas_call x1, Pallas kernels, shards(): pl.pallas_call(whole, out_shape=shapes, in_specs=[anywhere] * 19, out_spe...  136 us
    pallas_call x1, Pallas kernels, shards(): pl.pallas_call(hand_over, out_shape=shapes, in_specs=[anywhere] * 6, out_...  2.87 us

profile of v2, /device:TPU:1, one launch (start us, length us, event | category | flops | bytes accessed | tf_op | source)
XLA Modules:
  0.0 139.8 jit_solution(1402353844159896810)
XLA Ops:
  0.6 136.1 %shard_map.226 = (bf16[2,512,768]{2,1,0:T(8,128)(2,1)}, bf16[2,512,768]{2,1,0:T(8,128)(2,1)}, f32[1024]{0:T(1024)}, f32[768]{0:T(1024)}, f32[1024]{0:T(1024)}, /*index=5*/f32[768]{0:T(1024)}) custom-call(bf16[2,512,768]{2,1,0:T(8,128)(2,1)} %refs_0_.1, s32[2,1,8]{2,1,0:T(1,128)} %refs_1_.1, bf16[2,512,768]{2,1,0:T(8,128)(2,1)} %refs_2_.1, ...), custom_call_target="tpu_custom_call" | custom-call | tf_op jit(solution)/shard_map/pallas_call | solution.py:734
  136.7 2.9 %shard_map.227 = (bf16[2,512,768]{2,1,0:T(8,128)(2,1)}, bf16[2,512,768]{2,1,0:T(8,128)(2,1)}, f32[1024]{0:T(1024)}, f32[768]{0:T(1024)}, f32[1024]{0:T(1024)}, /*index=5*/f32[768]{0:T(1024)}) custom-call(bf16[2,512,768]{2,1,0:T(8,128)(2,1)} %get-tuple-element.12.refs_0_, bf16[2,512,768]{2,1,0:T(8,128)(2,1)} %get-tuple-element.13.refs_1_, ...), custom_call_target="tpu_custom_call" | custom-call | tf_op jit(solution)/shard_map/pallas_call | solution.py:743
